TPU v7x, 32 devices: a whole 2x2x4 slice. The times are simulated.
32 devices in a mesh: node: 4 (over z), local: 8 (over y, x, core).
Axes of the slice: x: 2, y: 2, z: 4, core: 2. Of those that a mesh axis runs over, the one named last changes fastest.
Arguments:
- tokens: bfloat16 [32, 3584], P(('node', 'local')), may hold values from -6 to 6
- out_grad: bfloat16 [32, 3584], P(('node', 'local')), may hold values from -2 to 2
- gate_prob: bfloat16 [32, 8], P(('node', 'local')), may hold values from 0.099609375 to 1
- dest_node: int32 [32, 8], P(('node', 'local')), may hold values from 0 to 3, as said below
- w_gate: bfloat16 [32, 3584, 1024], P(('node', 'local')), may hold values from -0.09375 to 0.09375
- w_up: bfloat16 [32, 3584, 1024], P(('node', 'local')), may hold values from -0.09375 to 0.09375
- w_down: bfloat16 [32, 1024, 3584], P(('node', 'local')), may hold values from -0.1875 to 0.1875
Outputs:
- in_grad: bfloat16 [32, 3584], P(('node', 'local'))
- gate_grad: float32 [32, 8], P(('node', 'local'))
Inputs may be any that keep to these rules, and one draw needn't show every extreme that they name: `dest_node`: columns 2 * g and 2 * g + 1 of a row are equal, so a token names at most half of 8 node groups, two experts in each. Among the 8 tokens of one node group, at most 4 name the same node group in one column; for each pair of columns one node group, the same for all source groups, is named by exactly 4 of them.
All inputs are finite; a program needn't handle non-finite values.
Results may differ from a plain program's by a relative error of at most 0.006.
Values may be sent and summed in bfloat16 or wider, within the bound.
A program may use at most 64 MiB of HBM per device.

v0:
```python
import jax
import jax.numpy as jnp
from jax import lax
from jax.sharding import PartitionSpec as P


def expert_terms(rows_x, rows_dy, rows_gate, weight_gate, weight_up, weight_down):
    contract = (((1,), (1,)), ((), ()))
    pre_gate = jnp.dot(rows_x, weight_gate, preferred_element_type=jnp.float32)
    pre_up = jnp.dot(rows_x, weight_up, preferred_element_type=jnp.float32)
    logistic = jax.nn.sigmoid(pre_gate)
    swished = pre_gate * logistic
    hidden = swished * pre_up
    back_hidden = lax.dot_general(
        rows_dy, weight_down, contract, preferred_element_type=jnp.float32
    )
    gate_terms = jnp.sum(hidden * back_hidden, axis=1)
    scaled = rows_gate[:, None] * back_hidden
    grad_gate = (scaled * pre_up * logistic * (1.0 + pre_gate * (1.0 - logistic))).astype(
        jnp.bfloat16
    )
    grad_up = (scaled * swished).astype(jnp.bfloat16)
    input_terms = lax.dot_general(
        grad_gate, weight_gate, contract, preferred_element_type=jnp.float32
    )
    input_terms = input_terms + lax.dot_general(
        grad_up, weight_up, contract, preferred_element_type=jnp.float32
    )
    return (input_terms, gate_terms)


def on_device(tokens, out_grad, gate_prob, dest_node, w_gate, w_up, w_down):
    node_count = lax.axis_size("node")
    local_count = lax.axis_size("local")
    local_id = lax.axis_index("local")
    width = tokens.shape[1]
    experts_here = gate_prob.shape[1]
    shards = local_count // experts_here
    column = local_id // shards
    pick_float = (jnp.arange(experts_here) == column).astype(jnp.float32)
    dest_half = dest_node.astype(jnp.bfloat16)
    home_x, home_dy, home_gate, home_dest = (
        lax.all_gather(tokens, "local", axis=0, tiled=True),
        lax.all_gather(out_grad, "local", axis=0, tiled=True),
        lax.all_gather(gate_prob, "local", axis=0, tiled=True),
        lax.all_gather(dest_half, "local", axis=0, tiled=True),
    )
    members = home_x.shape[0]
    capacity = 2 * members // node_count
    slots = node_count * capacity
    target = jnp.sum(home_dest.astype(jnp.float32) * pick_float[None, :], axis=1).astype(jnp.int32)
    onehot_dest = (target[:, None] == jnp.arange(node_count)[None, :]).astype(jnp.int32)
    before = jnp.cumsum(onehot_dest, axis=0) - onehot_dest
    position = target * capacity + jnp.sum(before * onehot_dest, axis=1)
    place_half = (jnp.arange(slots)[:, None] == position[None, :]).astype(jnp.bfloat16)
    send_x = jnp.dot(place_half, home_x, preferred_element_type=jnp.float32).astype(jnp.bfloat16)
    send_dy = jnp.dot(place_half, home_dy, preferred_element_type=jnp.float32).astype(jnp.bfloat16)
    send_gate = jnp.dot(place_half, home_gate, preferred_element_type=jnp.float32).astype(
        jnp.bfloat16
    )
    weight_gate = w_gate[0]
    weight_up = w_up[0]
    weight_down = w_down[0]
    part_x = lax.all_to_all(
        send_x.reshape(node_count, capacity, width), "node", split_axis=0, concat_axis=0, tiled=True
    )
    part_dy = lax.all_to_all(
        send_dy.reshape(node_count, capacity, width),
        "node",
        split_axis=0,
        concat_axis=0,
        tiled=True,
    )
    part_gate = lax.all_to_all(
        send_gate.reshape(node_count, capacity, experts_here),
        "node",
        split_axis=0,
        concat_axis=0,
        tiled=True,
    )
    leading = part_x.shape[0]
    items = part_x.shape[1]
    count = leading * items
    rows_gate = jnp.sum(
        part_gate.reshape(count, experts_here).astype(jnp.float32) * pick_float[None, :], axis=1
    )
    input_terms, gate_terms = expert_terms(
        part_x.reshape(count, width),
        part_dy.reshape(count, width),
        rows_gate,
        weight_gate,
        weight_up,
        weight_down,
    )
    gate_cols = gate_terms[:, None] * pick_float[None, :]
    back_x = lax.all_to_all(
        input_terms.reshape(leading, items, width), "node", split_axis=0, concat_axis=0, tiled=True
    )
    back_gate = lax.all_to_all(
        gate_cols.reshape(leading, items, experts_here),
        "node",
        split_axis=0,
        concat_axis=0,
        tiled=True,
    )
    term_x = jnp.take(back_x.reshape(slots, width), position, axis=0)
    term_gate = jnp.take(back_gate.reshape(slots, experts_here), position, axis=0)
    summed_x, summed_gate = (
        lax.psum_scatter(term_x, "local", scatter_dimension=0, tiled=True),
        lax.psum_scatter(term_gate, "local", scatter_dimension=0, tiled=True),
    )
    return (summed_x.astype(jnp.bfloat16), summed_gate)


def solution(mesh):
    return jax.shard_map(
        on_device,
        mesh=mesh,
        in_specs=(
            P(("node", "local"), None),
            P(("node", "local"), None),
            P(("node", "local"), None),
            P(("node", "local"), None),
            P(("node", "local"), None, None),
            P(("node", "local"), None, None),
            P(("node", "local"), None, None),
        ),
        out_specs=(P(("node", "local"), None), P(("node", "local"), None)),
        check_vma=False,
    )
```

profile of v0, /device:TPU:0, one launch (start us, length us, event | category | flops | bytes accessed | tf_op | source)
XLA Modules:
  0.0 119.8 jit_solution(13038224692575076213)
XLA Ops:
  1.3 10.2 %all-gather = bf16[8,1,8]{2,1,0:T(2,128)(2,1)S(1)} all-gather(bf16[1,1,8]{2,1,0:T(2,128)(2,1)S(1)} %convert_bitcast_fusion), channel_id=1, replica_groups=mesh['node'=4,'local'=8] {'local'}, dimensions={0}, use_global_device_ids=true | all-gather | bytes 144 | tf_op jit(solution)/shard_map/all_gather | solution.py:46
  11.8 9.2 %all-gather.3 = bf16[8,1,3584]{2,1,0:T(2,128)(2,1)S(1)} all-gather(bf16[1,1,3584]{2,1,0:T(2,128)(2,1)} %bitcast.47), channel_id=1, replica_groups=mesh['node'=4,'local'=8] {'local'}, dimensions={0}, use_global_device_ids=true | all-gather | bytes 64512 | tf_op jit(solution)/shard_map/all_gather | solution.py:43
  21.2 0.7 reshape.102
  21.9 4.9 %all-to-all-start.2 = ((bf16[4,4,3584]{2,1,0:T(4,128)(2,1)}), bf16[4,4,3584]{2,1,0:T(4,128)(2,1)S(1)}, u32[]{:S(2)}, u32[]{:S(2)}) async-start(bf16[4,4,3584]{2,1,0:T(4,128)(2,1)} %reshape.102), calls=%async_computation.2 | async-start | bytes 229376 | tf_op jit(solution)/shard_map/all_to_all | solution.py:64
  26.8 7.9 %all-gather.1 = bf16[8,1,8]{2,1,0:T(2,128)(2,1)S(1)} all-gather(bf16[1,1,8]{2,1,0:T(2,128)(2,1)} %bitcast.49), channel_id=1, replica_groups=mesh['node'=4,'local'=8] {'local'}, dimensions={0}, use_global_device_ids=true | all-gather | bytes 144 | tf_op jit(solution)/shard_map/all_gather | solution.py:45
  34.9 0.7 copy.14
  35.5 9.0 %all-gather.2 = bf16[8,1,3584]{2,1,0:T(2,128)(2,1)S(1)} all-gather(bf16[1,1,3584]{2,1,0:T(2,128)(2,1)} %bitcast.48), channel_id=1, replica_groups=mesh['node'=4,'local'=8] {'local'}, dimensions={0}, use_global_device_ids=true | all-gather | bytes 64512 | tf_op jit(solution)/shard_map/all_gather | solution.py:44
  44.7 0.7 reshape.100
  45.4 5.1 %all-to-all-start.1 = ((bf16[4,4,3584]{2,1,0:T(4,128)(2,1)}), bf16[4,4,3584]{2,1,0:T(4,128)(2,1)S(1)}, u32[]{:S(2)}, u32[]{:S(2)}) async-start(bf16[4,4,3584]{2,1,0:T(4,128)(2,1)} %reshape.100), calls=%async_computation.1 | async-start | bytes 229376 | tf_op jit(solution)/shard_map/all_to_all | solution.py:67
  50.6 4.3 %fusion.2 = f32[16,1024]{1,0:T(8,128)S(1)} fusion(bf16[16,3584]{1,0:T(8,128)(2,1)S(1)} %reshape.103, bf16[1,3584,1024]{2,1,0:T(8,128)(2,1)} %param.11), kind=kOutput, calls=%fused_computation.4 | convolution fusion | flops 117440512 | bytes 7520256 | tf_op jit(solution)/shard_map/dot_general | solution.py:9
  54.8 0.9 copy-done
  55.7 1.1 fusion.6
  56.8 5.1 %all-to-all-start = ((bf16[4,4,8]{2,1,0:T(4,128)(2,1)}), bf16[4,4,8]{2,1,0:T(4,128)(2,1)S(1)}, u32[]{:S(2)}, u32[]{:S(2)}) async-start(bf16[4,4,8]{2,1,0:T(4,128)(2,1)} %bitcast.3), calls=%async_computation | async-start | bytes 8192 | tf_op jit(solution)/shard_map/all_to_all | solution.py:74
  61.9 5.3 %multiply_reduce_fusion = (f32[16]{0:T(128)S(1)}, f32[16,1024]{1,0:T(8,128)S(1)}) fusion(f32[16,1024]{1,0:T(8,128)S(1)} %fusion.6, f32[16,1024]{1,0:T(8,128)S(1)} %fusion.2, bf16[16,3584]{1,0:T(8,128)(2,1)S(1)} %reshape.101, bf16[1,1024,3584]{2,1,0:T(8,128)(2,1)} %param.13), kind=kOutput, calls=%fused_computation.16 | convolution fusion | flops 117555184 | bytes 7651392 | tf_op jit(solution)/shard_map/dot_general | solution.py:14
  67.5 0.7 broadcast_multiply_fusion
  68.2 5.0 %all-to-all-start.4 = ((f32[4,4,8]{2,1,0:T(4,128)}), f32[4,4,8]{2,1,0:T(4,128)S(1)}, u32[]{:S(2)}, u32[]{:S(2)}) async-start(f32[4,4,8]{2,1,0:T(4,128)} %get-tuple-element.6), calls=%async_computation.4 | async-start | bytes 16384 | tf_op jit(solution)/shard_map/all_to_all | solution.py:99
  73.3 5.2 %fusion = f32[16,3584]{1,0:T(8,128)S(1)} fusion(bf16[1,3584,1024]{2,1,0:T(8,128)(2,1)} %param.11, f32[16,1024]{1,0:T(8,128)S(1)} %fusion.2, f32[16,1024]{1,0:T(8,128)S(1)} %fusion.6, f32[16,1024]{1,0:T(8,128)S(1)} %get-tuple-element.9, f32[16]{0:T(128)S(1)} %mul.91), kind=kOutput, calls=%fused_computation.2 | convolution fusion | flops 117620736 | bytes 7766080 | tf_op jit(solution)/shard_map/dot_general | solution.py:23
  78.5 2.0 %fusion.10 = f32[16,3584]{1,0:T(8,128)S(1)} fusion(f32[16,3584]{1,0:T(8,128)S(1)} %fusion, bf16[1,3584,1024]{2,1,0:T(8,128)(2,1)S(1)} %bitcast.45, f32[16,1024]{1,0:T(8,128)S(1)} %get-tuple-element.9, f32[16]{0:T(128)S(1)} %mul.91, f32[16,1024]{1,0:T(8,128)S(1)} %fusion.2), kind=kOutput, calls=%fused_computation.12 | convolution fusion | flops 117612544 | bytes 7929920 | tf_op jit(solution)/shard_map/dot_general | solution.py:26
  80.5 0.8 reshape.104
  81.3 5.1 %all-to-all-start.3 = ((f32[4,4,3584]{2,1,0:T(4,128)}), f32[4,4,3584]{2,1,0:T(4,128)S(1)}, u32[]{:S(2)}, u32[]{:S(2)}) async-start(f32[4,4,3584]{2,1,0:T(4,128)} %reshape.104), calls=%async_computation.3 | async-start | bytes 458752 | tf_op jit(solution)/shard_map/all_to_all | solution.py:96
  87.6 5.4 %all-to-all-done.3 = f32[4,4,3584]{2,1,0:T(4,128)S(1)} async-done(((f32[4,4,3584]{2,1,0:T(4,128)}), f32[4,4,3584]{2,1,0:T(4,128)S(1)}, u32[]{:S(2)}, u32[]{:S(2)}) %all-to-all-start.3) | async-done | bytes 229408 | tf_op jit(solution)/shard_map/all_to_all | solution.py:96
  93.8 23.6 %all-reduce.2 = (bf16[8,3584]{1,0:T(8,128)(2,1)S(1)}, f32[8,8]{1,0:T(8,128)S(1)}) all-reduce(f32[8,3584]{1,0:T(8,128)S(1)} %broadcast_select_fusion, f32[8,8]{1,0:T(8,128)S(1)} %broadcast_select_fusion.1), channel_id=2, replica_groups=mesh['node'=4,'local'=8] {'local'}, use_global_device_ids=true, to_apply=%region_4.5.clone | all-reduce | flops 28736 | bytes 172544
  117.4 1.3 %dynamic-slice_convert_fusion = bf16[1,3584]{1,0:T(2,128)(2,1)} fusion(bf16[8,3584]{1,0:T(8,128)(2,1)S(1)} %get-tuple-element.2, u32[]{:T(128)} %bitcast.13), kind=kLoop, calls=%fused_computation.29 | loop fusion | bytes 14340 | tf_op jit(solution)/shard_map/convert_element_type | solution.py:112
  118.7 1.1 constant_dynamic-slice_fusion
  (35 shorter events, 3.9 us)
Async XLA Ops:
  21.9 23.5 %all-to-all-start.2 = ((bf16[4,4,3584]{2,1,0:T(4,128)(2,1)}), bf16[4,4,3584]{2,1,0:T(4,128)(2,1)S(1)}, u32[]{:S(2)}, u32[]{:S(2)}) async-start(bf16[4,4,3584]{2,1,0:T(4,128)(2,1)} %reshape.102), calls=%async_computation.2 | async-start | bytes 229376 | tf_op jit(solution)/shard_map/all_to_all | solution.py:64
  45.4 11.4 %all-to-all-start.1 = ((bf16[4,4,3584]{2,1,0:T(4,128)(2,1)}), bf16[4,4,3584]{2,1,0:T(4,128)(2,1)S(1)}, u32[]{:S(2)}, u32[]{:S(2)}) async-start(bf16[4,4,3584]{2,1,0:T(4,128)(2,1)} %reshape.100), calls=%async_computation.1 | async-start | bytes 229376 | tf_op jit(solution)/shard_map/all_to_all | solution.py:67
  50.5 5.2 %copy-start = (bf16[1,3584,1024]{2,1,0:T(8,128)(2,1)S(1)}, bf16[1,3584,1024]{2,1,0:T(8,128)(2,1)}, u32[]{:S(2)}) copy-start(bf16[1,3584,1024]{2,1,0:T(8,128)(2,1)} %param.12) | copy-start | bytes 22020100
  56.8 10.7 %all-to-all-start = ((bf16[4,4,8]{2,1,0:T(4,128)(2,1)}), bf16[4,4,8]{2,1,0:T(4,128)(2,1)S(1)}, u32[]{:S(2)}, u32[]{:S(2)}) async-start(bf16[4,4,8]{2,1,0:T(4,128)(2,1)} %bitcast.3), calls=%async_computation | async-start | bytes 8192 | tf_op jit(solution)/shard_map/all_to_all | solution.py:74
  61.9 16.6 %slice-start = ((s8[7340032]{0:T(1024)(128)(4,1)}), s8[3145728]{0:T(1024)(128)(4,1)S(1)}, s32[]{:S(2)}) async-start(s8[7340032]{0:T(1024)(128)(4,1)} %bitcast.44), calls=%async_computation.5 | async-start | bytes 6291456
  68.2 13.1 %all-to-all-start.4 = ((f32[4,4,8]{2,1,0:T(4,128)}), f32[4,4,8]{2,1,0:T(4,128)S(1)}, u32[]{:S(2)}, u32[]{:S(2)}) async-start(f32[4,4,8]{2,1,0:T(4,128)} %get-tuple-element.6), calls=%async_computation.4 | async-start | bytes 16384 | tf_op jit(solution)/shard_map/all_to_all | solution.py:99
  73.3 5.2 %slice-start.1 = ((s8[7340032]{0:T(1024)(128)(4,1)}), s8[4194304]{0:T(1024)(128)(4,1)S(1)}, s32[]{:S(2)}) async-start(s8[7340032]{0:T(1024)(128)(4,1)} %bitcast.44), calls=%async_computation.6 | async-start | bytes 8388608
  73.3 13.1 %copy-start.1 = (u32[32]{0:T(128)S(1)}, u32[32]{0:T(128)}, u32[]{:S(2)}) copy-start(u32[32]{0:T(128)} %constant.63) | copy-start | bytes 388
  81.3 11.8 %all-to-all-start.3 = ((f32[4,4,3584]{2,1,0:T(4,128)}), f32[4,4,3584]{2,1,0:T(4,128)S(1)}, u32[]{:S(2)}, u32[]{:S(2)}) async-start(f32[4,4,3584]{2,1,0:T(4,128)} %reshape.104), calls=%async_computation.3 | async-start | bytes 458752 | tf_op jit(solution)/shard_map/all_to_all | solution.py:96
where the time goes:
time: 121 us; the launch traced here: 120 us
  blocking collectives  60 us (50%)
  starting transfers between devices  25.2 us (21%)
  matrix products  18.4 us (15%)
  local copies, waits for them, and re-layouts  8.14 us (7%)
  waiting for transfers between devices  5.52 us (5%)
  other arithmetic  1.88 us (2%)
    unnamed x1, blocking collectives  23.6 us
    all_gather x1, blocking collectives, on_device(): lax.all_gather(dest_half, 'local', axis=0, tiled=True)  10.2 us
    all_gather x1, blocking collectives, on_device(): lax.all_gather(tokens, 'local', axis=0, tiled=True)  9.21 us
    all_gather x1, blocking collectives, on_device(): lax.all_gather(out_grad, 'local', axis=0, tiled=True)  9.04 us
    all_gather x1, blocking collectives, on_device(): lax.all_gather(gate_prob, 'local', axis=0, tiled=True)  7.92 us
    all_to_all x1, waiting for transfers between devices, on_device(): lax.all_to_all(input_terms.reshape(leading, items, width), 'node', split_...  5.42 us
    dot_general x1, matrix products, expert_terms(): lax.dot_general(rows_dy, weight_down, contract, preferred_element_type=jn...  5.34 us
    dot_general x1, matrix products, expert_terms(): lax.dot_general(grad_gate, weight_gate, contract, preferred_element_type=...  5.24 us
  transfers between devices with their start and end apart: 5, of which 2 were waited for; matrix products, arithmetic and copies ran while one was open for 18% of the time, Pallas kernels for 0%

commit v1 on v0

v1 whole, which is shorter than its diff:
```python
import functools

import jax
import jax.numpy as jnp
from jax import lax
from jax.experimental import pallas as pl
from jax.experimental.pallas import tpu as pltpu
from jax.sharding import PartitionSpec as P

MESH = pl.DeviceIdType.MESH
LANES = 128
TILE = 256
HALVES = 2


def expert_terms(rows_x, rows_dy, rows_gate, weight_gate, weight_up, weight_down):
    contract = (((1,), (1,)), ((), ()))
    pre_gate = jnp.dot(rows_x, weight_gate, preferred_element_type=jnp.float32)
    pre_up = jnp.dot(rows_x, weight_up, preferred_element_type=jnp.float32)
    logistic = jax.nn.sigmoid(pre_gate)
    swished = pre_gate * logistic
    hidden = swished * pre_up
    back_hidden = lax.dot_general(
        rows_dy, weight_down, contract, preferred_element_type=jnp.float32
    )
    gate_terms = jnp.sum(hidden * back_hidden, axis=1)
    scaled = rows_gate[:, None] * back_hidden
    grad_gate = (scaled * pre_up * logistic * (1.0 + pre_gate * (1.0 - logistic))).astype(
        jnp.bfloat16
    )
    grad_up = (scaled * swished).astype(jnp.bfloat16)
    input_terms = lax.dot_general(
        grad_gate, weight_gate, contract, preferred_element_type=jnp.float32
    )
    input_terms = input_terms + lax.dot_general(
        grad_up, weight_up, contract, preferred_element_type=jnp.float32
    )
    return (input_terms, gate_terms)


def routed(tokens, out_grad, gate_prob, dest_node, w_gate, w_up, w_down):
    node_count = lax.axis_size("node")
    local_count = lax.axis_size("local")
    local_id = lax.axis_index("local")
    width = tokens.shape[1]
    experts_here = gate_prob.shape[1]
    shards = local_count // experts_here
    column = local_id // shards
    pick_float = (jnp.arange(experts_here) == column).astype(jnp.float32)
    dest_half = dest_node.astype(jnp.bfloat16)
    home_x, home_dy, home_gate, home_dest = (
        lax.all_gather(tokens, "local", axis=0, tiled=True),
        lax.all_gather(out_grad, "local", axis=0, tiled=True),
        lax.all_gather(gate_prob, "local", axis=0, tiled=True),
        lax.all_gather(dest_half, "local", axis=0, tiled=True),
    )
    members = home_x.shape[0]
    capacity = 2 * members // node_count
    slots = node_count * capacity
    target = jnp.sum(home_dest.astype(jnp.float32) * pick_float[None, :], axis=1).astype(jnp.int32)
    onehot_dest = (target[:, None] == jnp.arange(node_count)[None, :]).astype(jnp.int32)
    before = jnp.cumsum(onehot_dest, axis=0) - onehot_dest
    position = target * capacity + jnp.sum(before * onehot_dest, axis=1)
    place_half = (jnp.arange(slots)[:, None] == position[None, :]).astype(jnp.bfloat16)
    send_x = jnp.dot(place_half, home_x, preferred_element_type=jnp.float32).astype(jnp.bfloat16)
    send_dy = jnp.dot(place_half, home_dy, preferred_element_type=jnp.float32).astype(jnp.bfloat16)
    send_gate = jnp.dot(place_half, home_gate, preferred_element_type=jnp.float32).astype(
        jnp.bfloat16
    )

    def over_node(rows):
        return lax.all_to_all(
            rows.reshape(node_count, -1, rows.shape[1]),
            "node",
            split_axis=0,
            concat_axis=0,
            tiled=True,
        ).reshape(rows.shape)

    part_x, part_dy, part_gate = over_node(send_x), over_node(send_dy), over_node(send_gate)
    rows_gate = jnp.sum(part_gate.astype(jnp.float32) * pick_float[None, :], axis=1)
    input_terms, gate_terms = expert_terms(
        part_x, part_dy, rows_gate, w_gate[0], w_up[0], w_down[0]
    )
    gate_cols = gate_terms[:, None] * pick_float[None, :]
    back_x, back_gate = over_node(input_terms), over_node(gate_cols)
    term_x = jnp.take(back_x, position, axis=0)
    term_gate = jnp.take(back_gate, position, axis=0)
    summed_x, summed_gate = (
        lax.psum_scatter(term_x, "local", scatter_dimension=0, tiled=True),
        lax.psum_scatter(term_gate, "local", scatter_dimension=0, tiled=True),
    )
    return (summed_x.astype(jnp.bfloat16), summed_gate)


def dot_nt(a, b):
    return lax.dot_general(a, b, (((1,), (1,)), ((), ())), preferred_element_type=jnp.float32)


def fused_kernel(
    nodes,
    locals_,
    tok_ref,
    dy_ref,
    prob_ref,
    dest_ref,
    wg_hbm,
    wu_hbm,
    wd_hbm,
    out_ref,
    gate_ref,
    wg,
    wu,
    wd,
    stage,
    gath,
    wide,
    x_rows,
    dy_rows,
    dg,
    du,
    terms,
    send1,
    recv1,
    part,
    recv2,
    w_sem,
    zs,
    zr,
    cs,
    cr,
    ks,
    kr,
    ls,
    lr,
    bs,
    br,
):
    f32, bf16 = jnp.float32, jnp.bfloat16
    node, me = lax.axis_index("node"), lax.axis_index("local")
    chips = locals_ // 2
    chip, core = me // 2, me % 2
    sibling = chip * 2 + (1 - core)
    width = tok_ref.shape[1]
    units = wg.shape[1]
    half = width // HALVES
    rows = half // LANES
    padded = send1.shape[2] // nodes
    count = nodes * locals_

    loads = [
        pltpu.make_async_copy(src.at[0], dst, w_sem.at[i])
        for i, (src, dst) in enumerate(((wg_hbm, wg), (wu_hbm, wu), (wd_hbm, wd)))
    ]
    barrier = pltpu.get_barrier_semaphore()
    for k in range(1, nodes):
        pl.semaphore_signal(
            barrier, inc=1, device_id=((node + k) % nodes, me), device_id_type=MESH
        )
    for k in range(1, locals_):
        pl.semaphore_signal(
            barrier, inc=1, device_id=(node, (me + k) % locals_), device_id_type=MESH
        )
    for load in loads:
        load.start()

    stage[...] = jnp.zeros_like(stage)
    for at, ref in enumerate((tok_ref, dy_ref)):
        for h in range(HALVES):
            base = (at * HALVES + h) * padded
            for c in range(rows):
                lane = h * half + c * LANES
                stage[base + c : base + c + 1, :] = ref[:, lane : lane + LANES].astype(f32)
    experts = prob_ref.shape[1]
    stage[rows : rows + 1, 0:experts] = prob_ref[...].astype(f32)
    stage[rows + 1 : rows + 2, 0:experts] = dest_ref[...].astype(f32)
    gath[me, node] = stage[...].astype(bf16)
    pl.semaphore_wait(barrier, nodes - 1 + locals_ - 1)

    sent = []

    def send(src, dst, s_sem, r_sem, to):
        copy = pltpu.make_async_remote_copy(
            src_ref=src,
            dst_ref=dst,
            send_sem=s_sem,
            recv_sem=r_sem,
            device_id=to,
            device_id_type=MESH,
        )
        copy.start()
        sent.append(copy)

    def await_recv(ref, s_sem, r_sem):
        pltpu.make_async_remote_copy(
            src_ref=ref,
            dst_ref=ref,
            send_sem=s_sem,
            recv_sem=r_sem,
            device_id=(node, sibling),
            device_id_type=MESH,
        ).wait_recv()

    def spread(n, k):
        block = gath.at[me, n]
        for j in range(1, chips):
            to = ((chip + j) % chips) * 2 + core
            send(block, block, cs.at[k, j], cr.at[chip, n], (node, to))
        send(block, block, ks.at[k, 0], kr.at[chip, n], (node, sibling))

    own = gath.at[me, node]
    for k in range(1, nodes):
        send(own, own, zs.at[k], zr.at[node], ((node + k) % nodes, me))
    spread(node, 0)
    for k in range(1, nodes):
        n = (node + nodes - k) % nodes
        await_recv(gath.at[me, n], zs.at[0], zr.at[n])
        spread(n, k)
    for k in range(nodes):
        n = (node + nodes - k) % nodes
        for j in range(1, chips):
            other = (chip + chips - j) % chips
            block = gath.at[other * 2 + core, n]
            await_recv(block, cs.at[0, 0], cr.at[other, n])
            send(block, block, ks.at[k, j], kr.at[other, n], (node, sibling))
    for k in range(nodes):
        n = (node + nodes - k) % nodes
        for j in range(chips):
            other = (chip + chips - j) % chips
            await_recv(gath.at[other * 2 + 1 - core, n], ks.at[0, 0], kr.at[other, n])

    depth = 2 * HALVES * padded
    for l in range(locals_):
        for n in range(nodes):
            at = (l * nodes + n) * depth
            wide[at : at + depth, :] = gath[l, n].astype(f32)
    for at, ref in enumerate((x_rows, dy_rows)):
        for h in range(HALVES):
            for c in range(rows):
                lane = h * half + c * LANES
                first = (at * HALVES + h) * padded + c
                ref[:, lane : lane + LANES] = wide[pl.ds(first, count, stride=depth), :].astype(
                    bf16
                )
    lane_id = lax.broadcasted_iota(jnp.int32, (count, LANES), 1)
    mine = lane_id == me
    probs = wide[pl.ds(rows, count, stride=depth), :]
    dests = wide[pl.ds(rows + 1, count, stride=depth), :]
    prob = jnp.sum(jnp.where(mine, probs, 0.0), axis=1, keepdims=True)
    dest = jnp.sum(jnp.where(mine, dests, 0.0), axis=1, keepdims=True)
    here = dest == node.astype(f32)
    prob = jnp.where(here, prob, 0.0)

    for load in loads:
        load.wait()

    def hidden_tile(i, gate_sum):
        at = pl.ds(pl.multiple_of(i * TILE, TILE), TILE)
        pre_gate = jnp.dot(x_rows[...], wg[:, at], preferred_element_type=f32)
        pre_up = jnp.dot(x_rows[...], wu[:, at], preferred_element_type=f32)
        back = dot_nt(dy_rows[...], wd[at, :])
        logistic = jax.nn.sigmoid(pre_gate)
        swished = pre_gate * logistic
        gate_sum = gate_sum + jnp.sum(swished * pre_up * back, axis=1, keepdims=True)
        scaled = prob * back
        dg[:, at] = (scaled * pre_up * logistic * (1.0 + pre_gate * (1.0 - logistic))).astype(bf16)
        du[:, at] = (scaled * swished).astype(bf16)
        return gate_sum

    gate_sum = lax.fori_loop(0, units // TILE, hidden_tile, jnp.zeros((count, 1), f32))
    gate_row = jnp.where(mine & here, gate_sum, 0.0)
    gate_high = gate_row.astype(bf16).astype(f32)

    for h in range(HALVES):
        for extra in range(rows, padded):
            value = jnp.zeros((count, LANES), f32)
            if h == 0 and extra == rows:
                value = gate_high
            if h == 0 and extra == rows + 1:
                value = gate_row - gate_high
            terms[pl.ds(extra, count, stride=padded), :] = value

        def input_tile(i, _):
            at = pl.ds(pl.multiple_of(h * half + i * TILE, TILE), TILE)
            block = dot_nt(dg[...], wg[at, :]) + dot_nt(du[...], wu[at, :])
            for c in range(TILE // LANES):
                terms[pl.ds(i * (TILE // LANES) + c, count, stride=padded), :] = block[
                    :, c * LANES : (c + 1) * LANES
                ]
            return 0

        lax.fori_loop(0, half // TILE, input_tile, 0)
        for l in range(locals_):
            at = l * nodes * padded
            send1[h, l] = terms[at : at + nodes * padded, :].astype(bf16)
        for k in range(1, locals_):
            to = (me + k) % locals_
            send(send1.at[h, to], recv1.at[h, me], ls.at[h, k], lr.at[h, me], (node, to))

    for h in range(HALVES):
        total = send1[h, me].astype(f32)
        for k in range(1, locals_):
            source = (me + locals_ - k) % locals_
            await_recv(recv1.at[h, source], ls.at[h, 0], lr.at[h, source])
            total = total + recv1[h, source].astype(f32)
        for n in range(nodes):
            part[h, n] = total[n * padded : (n + 1) * padded]
        for k in range(1, nodes):
            to = (node + k) % nodes
            send(part.at[h, to], recv2.at[h, node], bs.at[h, k], br.at[h, node], (to, me))
    for h in range(HALVES):
        total = part[h, node]
        for k in range(1, nodes):
            source = (node + nodes - k) % nodes
            await_recv(recv2.at[h, source], bs.at[h, 0], br.at[h, source])
            total = total + recv2[h, source]
        for c in range(rows):
            lane = h * half + c * LANES
            out_ref[:, lane : lane + LANES] = total[c : c + 1].astype(bf16)
        if h == 0:
            gate_ref[...] = (total[rows : rows + 1] + total[rows + 1 : rows + 2])[:, 0:experts]
    for copy in sent:
        copy.wait_send()


def fused(nodes, locals_, tokens, out_grad, gate_prob, dest_node, w_gate, w_up, w_down):
    f32, bf16 = jnp.float32, jnp.bfloat16
    width, units = w_gate.shape[1:]
    count = nodes * locals_
    chips = locals_ // 2
    padded = padded_rows(width)
    depth = 2 * HALVES * padded
    vmem = pl.BlockSpec(memory_space=pltpu.VMEM)
    hbm = pl.BlockSpec(memory_space=pl.ANY)
    dma = pltpu.SemaphoreType.DMA
    return pl.pallas_call(
        functools.partial(fused_kernel, nodes, locals_),
        out_shape=(
            jax.ShapeDtypeStruct((1, width), bf16),
            jax.ShapeDtypeStruct(gate_prob.shape, f32),
        ),
        in_specs=[vmem] * 4 + [hbm] * 3,
        out_specs=(vmem, vmem),
        scratch_shapes=[
            pltpu.VMEM((width, units), bf16),
            pltpu.VMEM((width, units), bf16),
            pltpu.VMEM((units, width), bf16),
            pltpu.VMEM((depth, LANES), f32),
            pltpu.VMEM((locals_, nodes, depth, LANES), bf16),
            pltpu.VMEM((count * depth, LANES), f32),
            pltpu.VMEM((count, width), bf16),
            pltpu.VMEM((count, width), bf16),
            pltpu.VMEM((count, units), bf16),
            pltpu.VMEM((count, units), bf16),
            pltpu.VMEM((count * padded, LANES), f32),
            pltpu.VMEM((HALVES, locals_, nodes * padded, LANES), bf16),
            pltpu.VMEM((HALVES, locals_, nodes * padded, LANES), bf16),
            pltpu.VMEM((HALVES, nodes, padded, LANES), f32),
            pltpu.VMEM((HALVES, nodes, padded, LANES), f32),
            dma((3,)),
            dma((nodes,)),
            dma((nodes,)),
            dma((nodes, chips)),
            dma((chips, nodes)),
            dma((nodes, chips)),
            dma((chips, nodes)),
            dma((HALVES, locals_)),
            dma((HALVES, locals_)),
            dma((HALVES, nodes)),
            dma((HALVES, nodes)),
        ],
        compiler_params=pltpu.CompilerParams(
            collective_id=0, has_side_effects=True, vmem_limit_bytes=56 << 20
        ),
        cost_estimate=pl.CostEstimate(
            flops=10 * count * width * units,
            bytes_accessed=6 * width * units,
            transcendentals=count * units,
        ),
    )(tokens, out_grad, gate_prob, dest_node, w_gate, w_up, w_down)


def padded_rows(width):
    return -(-(width // HALVES // LANES + 2) // 16) * 16


def on_device(nodes, locals_, tokens, out_grad, gate_prob, dest_node, w_gate, w_up, w_down):
    width, units = w_gate.shape[1:]
    weights = 6 * width * units
    rows = nodes * locals_ * 2 * HALVES * padded_rows(width) * LANES * 10
    small = (
        tokens.shape[0] == 1
        and gate_prob.shape[1] == locals_
        and locals_ % 2 == 0
        and width % (HALVES * TILE) == 0
        and units % TILE == 0
        and weights + rows < 40 << 20
    )
    plan = functools.partial(fused, nodes, locals_) if small else routed
    return plan(tokens, out_grad, gate_prob, dest_node, w_gate, w_up, w_down)


def solution(mesh):
    split = ("node", "local")
    return jax.shard_map(
        functools.partial(on_device, mesh.shape["node"], mesh.shape["local"]),
        mesh=mesh,
        in_specs=(P(split, None),) * 4 + (P(split, None, None),) * 3,
        out_specs=(P(split, None), P(split, None)),
        check_vma=False,
    )
```

time: 121 us -> 38.4 us (0.32)
  blocking collectives: 60 us -> 0 us
  Pallas kernels: 0 us -> 35 us
  starting transfers between devices: 25.2 us -> 0 us
  matrix products: 18.4 us -> 0 us
  local copies, waits for them, and re-layouts: 8.14 us -> 2.46 us
  waiting for transfers between devices: 5.52 us -> 0 us
  other arithmetic: 1.88 us -> 0 us
    all_gather x4 -> x0, blocking collectives: 36.4 us -> none  [the longest x1 10.2 us: on_device(): lax.all_gather(dest_half, 'local', axis=0, tiled=True)]
    pallas_call x0 -> x1, Pallas kernels: none -> 35 us  [fused(): pl.pallas_call(functools.partial(fused_kernel, nodes, locals_), out_shape...]
    all_to_all x5 -> x0, starting transfers between devices: 25.2 us -> none  [the longest x1 5.1 us: on_device(): lax.all_to_all(send_gate.reshape(node_count, capacity, experts_here), 'no...]
    unnamed x1 -> x0, blocking collectives: 23.6 us -> none
    dot_general x8 -> x0, matrix products: 18.4 us -> none  [the longest x1 5.34 us: expert_terms(): lax.dot_general(rows_dy, weight_down, contract, preferred_element_type=jn...]
    all_to_all x5 -> x0, waiting for transfers between devices: 5.52 us -> none  [the longest x1 5.42 us: on_device(): lax.all_to_all(input_terms.reshape(leading, items, width), 'node', split_...]
    reshape x6 -> x0, local copies, waits for them, and re-layouts: 2.26 us -> none  [the longest x1 0.77 us: on_device(): input_terms.reshape(leading, items, width)]
    convert_element_type x2 -> x0, local copies, waits for them, and re-layouts: 1.93 us -> none  [the longest x1 1.25 us: on_device(): return (summed_x.astype(jnp.bfloat16), summed_gate)]
  transfers between devices with their start and end apart: 5 -> 0, of which waited for: 2 -> 0; matrix products, arithmetic and copies ran while one was open for 18% -> 0% of each run, Pallas kernels for 0% -> 0%
where the time goes in v1:
time: 38.4 us; the launch traced here: 38.1 us
  Pallas kernels  35 us (91%)
  local copies, waits for them, and re-layouts  2.46 us (6%)
  between operations  0.64 us (2%)
    pallas_call x1, Pallas kernels, fused(): pl.pallas_call(functools.partial(fused_kernel, nodes, locals_), out_shape...  35 us
    unnamed x2, local copies, waits for them, and re-layouts  2.46 us

profile of v1, /device:TPU:0, one launch (start us, length us, event | category | flops | bytes accessed | tf_op | source)
XLA Modules:
  0.0 38.1 jit_solution(12861115101987842395)
XLA Ops:
  0.6 35.0 %shard_map.86 = (bf16[1,3584]{1,0:T(2,128)(2,1)}, f32[1,8]{1,0:T(1,128)}) custom-call(bf16[1,3584]{1,0:T(2,128)(2,1)} %tok_ref.1, bf16[1,3584]{1,0:T(2,128)(2,1)} %dy_ref.1, bf16[1,8]{1,0:T(2,128)(2,1)} %prob_ref.1, s32[1,8]{1,0:T(1,128)} %dest_ref.1, bf16[1,3584,1024]{2,1,0:T(8,128)(2,1)} %wg_hbm.1, bf16[1,3584,1024]{2,1,0:T(8,128)(2,1)} %wu_hbm.1, ...), custom_call_target="tpu_custom_call" | custom-call | flops 1174405120 | bytes 22020096 | tf_op jit(solution)/shard_map/pallas_call | solution.py:336
  35.7 1.3 %copy.11 = bf16[1,3584]{1,0:T(2,128)(2,1)} copy(bf16[1,3584]{1,0:T(2,128)(2,1)} %get-tuple-element.4) | data formatting | bytes 14336
  37.0 1.1 %copy.12 = f32[1,8]{1,0:T(1,128)} copy(f32[1,8]{1,0:T(1,128)} %get-tuple-element.5) | data formatting | bytes 64

commit v2 on v1

--- a/solution.py
+++ b/solution.py
@@ -113,10 +113,12 @@
     wu,
     wd,
     stage,
-    gath,
+    gath_x,
+    gath_dy,
     wide,
-    x_rows,
-    dy_rows,
+    rows_ref,
+    pre_g,
+    pre_u,
     dg,
     du,
     terms,
@@ -131,6 +133,8 @@
     cr,
     ks,
     kr,
+    ds,
+    dr,
     ls,
     lr,
     bs,
@@ -140,13 +144,20 @@
     node, me = lax.axis_index("node"), lax.axis_index("local")
     chips = locals_ // 2
     chip, core = me // 2, me % 2
-    sibling = chip * 2 + (1 - core)
     width = tok_ref.shape[1]
     units = wg.shape[1]
     half = width // HALVES
     rows = half // LANES
-    padded = send1.shape[2] // nodes
+    padded = send1.shape[3] // nodes
     count = nodes * locals_
+    depth = HALVES * padded
+    peers = [(j, side) for j in range(chips) for side in range(2) if (j, side) != (0, 0)]
+
+    def ahead(j, side):
+        return (node, ((chip + j) % chips) * 2 + (core if side == 0 else 1 - core))
+
+    def back(j, side):
+        return (node, ((chip + chips - j) % chips) * 2 + (core if side == 0 else 1 - core))
 
     loads = [
         pltpu.make_async_copy(src.at[0], dst, w_sem.at[i])
@@ -157,30 +168,28 @@
         pl.semaphore_signal(
             barrier, inc=1, device_id=((node + k) % nodes, me), device_id_type=MESH
         )
-    for k in range(1, locals_):
-        pl.semaphore_signal(
-            barrier, inc=1, device_id=(node, (me + k) % locals_), device_id_type=MESH
-        )
+    for j, side in peers:
+        pl.semaphore_signal(barrier, inc=1, device_id=ahead(j, side), device_id_type=MESH)
     for load in loads:
         load.start()
 
-    stage[...] = jnp.zeros_like(stage)
-    for at, ref in enumerate((tok_ref, dy_ref)):
+    experts = prob_ref.shape[1]
+    for ref, gath in ((tok_ref, gath_x), (dy_ref, gath_dy)):
+        stage[...] = jnp.zeros_like(stage)
         for h in range(HALVES):
-            base = (at * HALVES + h) * padded
             for c in range(rows):
-                lane = h * half + c * LANES
-                stage[base + c : base + c + 1, :] = ref[:, lane : lane + LANES].astype(f32)
-    experts = prob_ref.shape[1]
-    stage[rows : rows + 1, 0:experts] = prob_ref[...].astype(f32)
-    stage[rows + 1 : rows + 2, 0:experts] = dest_ref[...].astype(f32)
-    gath[me, node] = stage[...].astype(bf16)
-    pl.semaphore_wait(barrier, nodes - 1 + locals_ - 1)
+                lane, at = h * half + c * LANES, h * padded + c
+                stage[at : at + 1, :] = ref[:, lane : lane + LANES].astype(f32)
+        if ref is tok_ref:
+            stage[rows : rows + 1, 0:experts] = prob_ref[...].astype(f32)
+            stage[rows + 1 : rows + 2, 0:experts] = dest_ref[...].astype(f32)
+        gath[0, 0, 0] = stage[...].astype(bf16)
+    pl.semaphore_wait(barrier, nodes - 1 + len(peers))
 
     sent = []
 
-    def send(src, dst, s_sem, r_sem, to):
-        copy = pltpu.make_async_remote_copy(
+    def remote(src, dst, s_sem, r_sem, to):
+        return pltpu.make_async_remote_copy(
             src_ref=src,
             dst_ref=dst,
             send_sem=s_sem,
@@ -188,60 +197,65 @@
             device_id=to,
             device_id_type=MESH,
         )
+
+    def send(src, dst, s_sem, r_sem, to):
+        copy = remote(src, dst, s_sem, r_sem, to)
         copy.start()
         sent.append(copy)
 
     def await_recv(ref, s_sem, r_sem):
-        pltpu.make_async_remote_copy(
-            src_ref=ref,
-            dst_ref=ref,
-            send_sem=s_sem,
-            recv_sem=r_sem,
-            device_id=(node, sibling),
-            device_id_type=MESH,
-        ).wait_recv()
-
-    def spread(n, k):
-        block = gath.at[me, n]
+        remote(ref, ref, s_sem, r_sem, ahead(0, 1)).wait_recv()
+
+    def across(k):
         for j in range(1, chips):
-            to = ((chip + j) % chips) * 2 + core
-            send(block, block, cs.at[k, j], cr.at[chip, n], (node, to))
-        send(block, block, ks.at[k, 0], kr.at[chip, n], (node, sibling))
-
-    own = gath.at[me, node]
+            send(gath_x.at[0, 0, k], gath_x.at[j, 0, k], cs.at[j, k], cr.at[j, k], ahead(j, 0))
+
+    def sideways(j):
+        send(gath_x.at[j, 0], gath_x.at[j, 1], ks.at[j], kr.at[j], ahead(0, 1))
+
+    for at, gath in enumerate((gath_x, gath_dy)):
+        for k in range(1, nodes):
+            to = ((node + k) % nodes, me)
+            send(gath.at[0, 0, 0], gath.at[0, 0, k], zs.at[at, k], zr.at[at, k], to)
+        if at == 0:
+            across(0)
     for k in range(1, nodes):
-        send(own, own, zs.at[k], zr.at[node], ((node + k) % nodes, me))
-    spread(node, 0)
+        await_recv(gath_x.at[0, 0, k], zs.at[0, 0], zr.at[0, k])
+        across(k)
+    sideways(0)
     for k in range(1, nodes):
-        n = (node + nodes - k) % nodes
-        await_recv(gath.at[me, n], zs.at[0], zr.at[n])
-        spread(n, k)
-    for k in range(nodes):
-        n = (node + nodes - k) % nodes
-        for j in range(1, chips):
-            other = (chip + chips - j) % chips
-            block = gath.at[other * 2 + core, n]
-            await_recv(block, cs.at[0, 0], cr.at[other, n])
-            send(block, block, ks.at[k, j], kr.at[other, n], (node, sibling))
-    for k in range(nodes):
-        n = (node + nodes - k) % nodes
-        for j in range(chips):
-            other = (chip + chips - j) % chips
-            await_recv(gath.at[other * 2 + 1 - core, n], ks.at[0, 0], kr.at[other, n])
-
-    depth = 2 * HALVES * padded
-    for l in range(locals_):
-        for n in range(nodes):
-            at = (l * nodes + n) * depth
-            wide[at : at + depth, :] = gath[l, n].astype(f32)
-    for at, ref in enumerate((x_rows, dy_rows)):
+        await_recv(gath_dy.at[0, 0, k], zs.at[0, 0], zr.at[1, k])
+    for j, side in peers:
+        send(
+            gath_dy.at[0, 0],
+            gath_dy.at[j, side],
+            ds.at[j, side],
+            dr.at[j, side],
+            ahead(j, side),
+        )
+    for j in range(1, chips):
+        for k in range(nodes):
+            await_recv(gath_x.at[j, 0, k], cs.at[0, 0], cr.at[j, k])
+        sideways(j)
+    for j in range(chips):
+        await_recv(gath_x.at[j, 1], ks.at[0], kr.at[j])
+
+    def to_rows(gath):
+        def widen(l, _):
+            block = gath[l // 2, l % 2].astype(f32).reshape(nodes * depth, LANES)
+            at = pl.multiple_of(l * (nodes * depth), nodes * depth)
+            wide[pl.ds(at, nodes * depth), :] = block
+            return 0
+
+        lax.fori_loop(0, locals_, widen, 0)
         for h in range(HALVES):
             for c in range(rows):
-                lane = h * half + c * LANES
-                first = (at * HALVES + h) * padded + c
-                ref[:, lane : lane + LANES] = wide[pl.ds(first, count, stride=depth), :].astype(
-                    bf16
-                )
+                lane, first = h * half + c * LANES, h * padded + c
+                rows_ref[:, lane : lane + LANES] = wide[
+                    pl.ds(first, count, stride=depth), :
+                ].astype(bf16)
+
+    to_rows(gath_x)
     lane_id = lax.broadcasted_iota(jnp.int32, (count, LANES), 1)
     mine = lane_id == me
     probs = wide[pl.ds(rows, count, stride=depth), :]
@@ -251,18 +265,30 @@
     here = dest == node.astype(f32)
     prob = jnp.where(here, prob, 0.0)
 
-    for load in loads:
-        load.wait()
+    loads[0].wait()
+    loads[1].wait()
+
+    def forward_tile(i, _):
+        at = pl.ds(pl.multiple_of(i * TILE, TILE), TILE)
+        pre_g[:, at] = jnp.dot(rows_ref[...], wg[:, at], preferred_element_type=f32)
+        pre_u[:, at] = jnp.dot(rows_ref[...], wu[:, at], preferred_element_type=f32)
+        return 0
+
+    lax.fori_loop(0, units // TILE, forward_tile, 0)
+
+    for j, side in peers:
+        await_recv(gath_dy.at[j, side], ds.at[0, 0], dr.at[j, side])
+    to_rows(gath_dy)
+    loads[2].wait()
 
     def hidden_tile(i, gate_sum):
         at = pl.ds(pl.multiple_of(i * TILE, TILE), TILE)
-        pre_gate = jnp.dot(x_rows[...], wg[:, at], preferred_element_type=f32)
-        pre_up = jnp.dot(x_rows[...], wu[:, at], preferred_element_type=f32)
-        back = dot_nt(dy_rows[...], wd[at, :])
+        pre_gate, pre_up = pre_g[:, at], pre_u[:, at]
+        back_hidden = dot_nt(rows_ref[...], wd[at, :])
         logistic = jax.nn.sigmoid(pre_gate)
         swished = pre_gate * logistic
-        gate_sum = gate_sum + jnp.sum(swished * pre_up * back, axis=1, keepdims=True)
-        scaled = prob * back
+        gate_sum = gate_sum + jnp.sum(swished * pre_up * back_hidden, axis=1, keepdims=True)
+        scaled = prob * back_hidden
         dg[:, at] = (scaled * pre_up * logistic * (1.0 + pre_gate * (1.0 - logistic))).astype(bf16)
         du[:, at] = (scaled * swished).astype(bf16)
         return gate_sum
@@ -290,30 +316,34 @@
             return 0
 
         lax.fori_loop(0, half // TILE, input_tile, 0)
-        for l in range(locals_):
-            at = l * nodes * padded
-            send1[h, l] = terms[at : at + nodes * padded, :].astype(bf16)
-        for k in range(1, locals_):
-            to = (me + k) % locals_
-            send(send1.at[h, to], recv1.at[h, me], ls.at[h, k], lr.at[h, me], (node, to))
+        for j in range(chips):
+            for side in range(2):
+                at = (j * 2 + side) * nodes * padded
+                send1[h, j, side] = terms[at : at + nodes * padded, :].astype(bf16)
+                if (j, side) != (0, 0):
+                    send(
+                        send1.at[h, j, side],
+                        recv1.at[h, j, side],
+                        ls.at[h, j, side],
+                        lr.at[h, j, side],
+                        back(j, side),
+                    )
 
     for h in range(HALVES):
-        total = send1[h, me].astype(f32)
-        for k in range(1, locals_):
-            source = (me + locals_ - k) % locals_
-            await_recv(recv1.at[h, source], ls.at[h, 0], lr.at[h, source])
-            total = total + recv1[h, source].astype(f32)
-        for n in range(nodes):
-            part[h, n] = total[n * padded : (n + 1) * padded]
+        total = send1[h, 0, 0].astype(f32)
+        for j, side in peers:
+            await_recv(recv1.at[h, j, side], ls.at[h, 0, 0], lr.at[h, j, side])
+            total = total + recv1[h, j, side].astype(f32)
+        for k in range(nodes):
+            part[h, k] = total[k * padded : (k + 1) * padded]
         for k in range(1, nodes):
-            to = (node + k) % nodes
-            send(part.at[h, to], recv2.at[h, node], bs.at[h, k], br.at[h, node], (to, me))
+            to = ((node + nodes - k) % nodes, me)
+            send(part.at[h, k], recv2.at[h, k], bs.at[h, k], br.at[h, k], to)
     for h in range(HALVES):
-        total = part[h, node]
+        total = part[h, 0]
         for k in range(1, nodes):
-            source = (node + nodes - k) % nodes
-            await_recv(recv2.at[h, source], bs.at[h, 0], br.at[h, source])
-            total = total + recv2[h, source]
+            await_recv(recv2.at[h, k], bs.at[h, 0], br.at[h, k])
+            total = total + recv2[h, k]
         for c in range(rows):
             lane = h * half + c * LANES
             out_ref[:, lane : lane + LANES] = total[c : c + 1].astype(bf16)
@@ -329,7 +359,7 @@
     count = nodes * locals_
     chips = locals_ // 2
     padded = padded_rows(width)
-    depth = 2 * HALVES * padded
+    depth = HALVES * padded
     vmem = pl.BlockSpec(memory_space=pltpu.VMEM)
     hbm = pl.BlockSpec(memory_space=pl.ANY)
     dma = pltpu.SemaphoreType.DMA
@@ -346,26 +376,30 @@
             pltpu.VMEM((width, units), bf16),
             pltpu.VMEM((units, width), bf16),
             pltpu.VMEM((depth, LANES), f32),
-            pltpu.VMEM((locals_, nodes, depth, LANES), bf16),
+            pltpu.VMEM((chips, 2, nodes, depth, LANES), bf16),
+            pltpu.VMEM((chips, 2, nodes, depth, LANES), bf16),
             pltpu.VMEM((count * depth, LANES), f32),
             pltpu.VMEM((count, width), bf16),
-            pltpu.VMEM((count, width), bf16),
+            pltpu.VMEM((count, units), f32),
+            pltpu.VMEM((count, units), f32),
             pltpu.VMEM((count, units), bf16),
             pltpu.VMEM((count, units), bf16),
             pltpu.VMEM((count * padded, LANES), f32),
-            pltpu.VMEM((HALVES, locals_, nodes * padded, LANES), bf16),
-            pltpu.VMEM((HALVES, locals_, nodes * padded, LANES), bf16),
+            pltpu.VMEM((HALVES, chips, 2, nodes * padded, LANES), bf16),
+            pltpu.VMEM((HALVES, chips, 2, nodes * padded, LANES), bf16),
             pltpu.VMEM((HALVES, nodes, padded, LANES), f32),
             pltpu.VMEM((HALVES, nodes, padded, LANES), f32),
             dma((3,)),
-            dma((nodes,)),
-            dma((nodes,)),
-            dma((nodes, chips)),
+            dma((2, nodes)),
+            dma((2, nodes)),
             dma((chips, nodes)),
-            dma((nodes, chips)),
             dma((chips, nodes)),
-            dma((HALVES, locals_)),
-            dma((HALVES, locals_)),
+            dma((chips,)),
+            dma((chips,)),
+            dma((chips, 2)),
+            dma((chips, 2)),
+            dma((HALVES, chips, 2)),
+            dma((HALVES, chips, 2)),
             dma((HALVES, nodes)),
             dma((HALVES, nodes)),
         ],

time: 38.4 us -> 38.9 us (1.013)
  Pallas kernels: 35 us -> 35.5 us
    pallas_call x1, Pallas kernels: 35 us -> 35.5 us  [fused(): pl.pallas_call(functools.partial(fused_kernel, nodes, locals_), out_shape...]
where the time goes in v2:
time: 38.9 us; the launch traced here: 38.6 us
  Pallas kernels  35.5 us (91%)
  local copies, waits for them, and re-layouts  2.46 us (6%)
  between operations  0.64 us (2%)
    pallas_call x1, Pallas kernels, fused(): pl.pallas_call(functools.partial(fused_kernel, nodes, locals_), out_shape...  35.5 us
    unnamed x2, local copies, waits for them, and re-layouts  2.46 us

profile of v2, /device:TPU:0, one launch (start us, length us, event | category | flops | bytes accessed | tf_op | source)
XLA Modules:
  0.0 38.6 jit_solution(9380559133344475037)
XLA Ops:
  0.6 35.5 %shard_map.86 = (bf16[1,3584]{1,0:T(2,128)(2,1)}, f32[1,8]{1,0:T(1,128)}) custom-call(bf16[1,3584]{1,0:T(2,128)(2,1)} %tok_ref.1, bf16[1,3584]{1,0:T(2,128)(2,1)} %dy_ref.1, bf16[1,8]{1,0:T(2,128)(2,1)} %prob_ref.1, s32[1,8]{1,0:T(1,128)} %dest_ref.1, bf16[1,3584,1024]{2,1,0:T(8,128)(2,1)} %wg_hbm.1, bf16[1,3584,1024]{2,1,0:T(8,128)(2,1)} %wu_hbm.1, ...), custom_call_target="tpu_custom_call" | custom-call | flops 1174405120 | bytes 22020096 | tf_op jit(solution)/shard_map/pallas_call | solution.py:366
  36.1 1.3 %copy.11 = bf16[1,3584]{1,0:T(2,128)(2,1)} copy(bf16[1,3584]{1,0:T(2,128)(2,1)} %get-tuple-element.4) | data formatting | bytes 14336
  37.4 1.1 %copy.12 = f32[1,8]{1,0:T(1,128)} copy(f32[1,8]{1,0:T(1,128)} %get-tuple-element.5) | data formatting | bytes 64

commit v3 on v2

--- a/solution.py
+++ b/solution.py
@@ -11,6 +11,7 @@
 LANES = 128
 TILE = 256
 HALVES = 2
+PIECES = 2
 
 
 def expert_terms(rows_x, rows_dy, rows_gate, weight_gate, weight_up, weight_down):
@@ -108,7 +109,6 @@
     wu_hbm,
     wd_hbm,
     out_ref,
-    gate_ref,
     wg,
     wu,
     wd,
@@ -159,10 +159,20 @@
     def back(j, side):
         return (node, ((chip + chips - j) % chips) * 2 + (core if side == 0 else 1 - core))
 
-    loads = [
-        pltpu.make_async_copy(src.at[0], dst, w_sem.at[i])
-        for i, (src, dst) in enumerate(((wg_hbm, wg), (wu_hbm, wu), (wd_hbm, wd)))
-    ]
+    def load(which, i, p):
+        src, dst = ((wg_hbm, wg), (wu_hbm, wu), (wd_hbm, wd))[which]
+        if which == 2:
+            step = TILE // PIECES
+            at = (pl.ds(pl.multiple_of(i * TILE + p * step, step), step), slice(None))
+        else:
+            step = width // PIECES
+            at = (pl.ds(p * step, step), pl.ds(pl.multiple_of(i * TILE, TILE), TILE))
+        return pltpu.make_async_copy(src.at[(0, *at)], dst.at[at], w_sem.at[which, i, p])
+
+    def await_load(which, i):
+        for p in range(PIECES):
+            load(which, i, p).wait()
+
     barrier = pltpu.get_barrier_semaphore()
     for k in range(1, nodes):
         pl.semaphore_signal(
@@ -170,8 +180,11 @@
         )
     for j, side in peers:
         pl.semaphore_signal(barrier, inc=1, device_id=ahead(j, side), device_id_type=MESH)
-    for load in loads:
-        load.start()
+    for group in ((0, 1), (2,)):
+        for i in range(units // TILE):
+            for which in group:
+                for p in range(PIECES):
+                    load(which, i, p).start()
 
     experts = prob_ref.shape[1]
     for ref, gath in ((tok_ref, gath_x), (dy_ref, gath_dy)):
@@ -265,10 +278,9 @@
     here = dest == node.astype(f32)
     prob = jnp.where(here, prob, 0.0)
 
-    loads[0].wait()
-    loads[1].wait()
-
     def forward_tile(i, _):
+        await_load(0, i)
+        await_load(1, i)
         at = pl.ds(pl.multiple_of(i * TILE, TILE), TILE)
         pre_g[:, at] = jnp.dot(rows_ref[...], wg[:, at], preferred_element_type=f32)
         pre_u[:, at] = jnp.dot(rows_ref[...], wu[:, at], preferred_element_type=f32)
@@ -279,9 +291,9 @@
     for j, side in peers:
         await_recv(gath_dy.at[j, side], ds.at[0, 0], dr.at[j, side])
     to_rows(gath_dy)
-    loads[2].wait()
 
     def hidden_tile(i, gate_sum):
+        await_load(2, i)
         at = pl.ds(pl.multiple_of(i * TILE, TILE), TILE)
         pre_gate, pre_up = pre_g[:, at], pre_u[:, at]
         back_hidden = dot_nt(rows_ref[...], wd[at, :])
@@ -344,11 +356,7 @@
         for k in range(1, nodes):
             await_recv(recv2.at[h, k], bs.at[h, 0], br.at[h, k])
             total = total + recv2[h, k]
-        for c in range(rows):
-            lane = h * half + c * LANES
-            out_ref[:, lane : lane + LANES] = total[c : c + 1].astype(bf16)
-        if h == 0:
-            gate_ref[...] = (total[rows : rows + 1] + total[rows + 1 : rows + 2])[:, 0:experts]
+        out_ref[h] = total
     for copy in sent:
         copy.wait_send()
 
@@ -363,14 +371,11 @@
     vmem = pl.BlockSpec(memory_space=pltpu.VMEM)
     hbm = pl.BlockSpec(memory_space=pl.ANY)
     dma = pltpu.SemaphoreType.DMA
-    return pl.pallas_call(
+    total = pl.pallas_call(
         functools.partial(fused_kernel, nodes, locals_),
-        out_shape=(
-            jax.ShapeDtypeStruct((1, width), bf16),
-            jax.ShapeDtypeStruct(gate_prob.shape, f32),
-        ),
+        out_shape=jax.ShapeDtypeStruct((HALVES, padded, LANES), f32),
         in_specs=[vmem] * 4 + [hbm] * 3,
-        out_specs=(vmem, vmem),
+        out_specs=vmem,
         scratch_shapes=[
             pltpu.VMEM((width, units), bf16),
             pltpu.VMEM((width, units), bf16),
@@ -389,7 +394,7 @@
             pltpu.VMEM((HALVES, chips, 2, nodes * padded, LANES), bf16),
             pltpu.VMEM((HALVES, nodes, padded, LANES), f32),
             pltpu.VMEM((HALVES, nodes, padded, LANES), f32),
-            dma((3,)),
+            dma((3, units // TILE, PIECES)),
             dma((2, nodes)),
             dma((2, nodes)),
             dma((chips, nodes)),
@@ -412,6 +417,25 @@
             transcendentals=count * units,
         ),
     )(tokens, out_grad, gate_prob, dest_node, w_gate, w_up, w_down)
+    return pl.pallas_call(
+        round_kernel,
+        out_shape=(
+            jax.ShapeDtypeStruct((1, width), bf16),
+            jax.ShapeDtypeStruct(gate_prob.shape, f32),
+        ),
+        in_specs=[vmem],
+        out_specs=(vmem, vmem),
+    )(total)
+
+
+def round_kernel(total_ref, out_ref, gate_ref):
+    rows = out_ref.shape[1] // HALVES // LANES
+    for h in range(HALVES):
+        for c in range(rows):
+            lane = (h * rows + c) * LANES
+            out_ref[:, lane : lane + LANES] = total_ref[h, c : c + 1].astype(jnp.bfloat16)
+    gate = total_ref[0, rows : rows + 1] + total_ref[0, rows + 1 : rows + 2]
+    gate_ref[...] = gate[:, 0 : gate_ref.shape[1]]
 
 
 def padded_rows(width):

time: 38.9 us -> 38 us (0.977)
  local copies, waits for them, and re-layouts: 2.46 us -> 0 us
  Pallas kernels: 35.5 us -> 37 us
    unnamed x2 -> x0, local copies, waits for them, and re-layouts: 2.46 us -> none
    pallas_call x0 -> x1, Pallas kernels: none -> 1.34 us  [fused(): pl.pallas_call(round_kernel, out_shape=(jax.ShapeDtypeStruct((1, width),...]
where the time goes in v3:
time: 38 us; the launch traced here: 37.7 us
  Pallas kernels  37 us (97%)
  between operations  0.64 us (2%)
    pallas_call x1, Pallas kernels, fused(): pl.pallas_call(functools.partial(fused_kernel, nodes, locals_), out_shape...  35.7 us
    pallas_call x1, Pallas kernels, fused(): pl.pallas_call(round_kernel, out_shape=(jax.ShapeDtypeStruct((1, width),...  1.34 us

profile of v3, /device:TPU:0, one launch (start us, length us, event | category | flops | bytes accessed | tf_op | source)
XLA Modules:
  0.0 37.7 jit_solution(12422776774872744924)
XLA Ops:
  0.6 35.7 %shard_map.86.total_ref = f32[2,16,128]{2,1,0:T(8,128)} custom-call(bf16[1,3584]{1,0:T(2,128)(2,1)} %tok_ref.1, bf16[1,3584]{1,0:T(2,128)(2,1)} %dy_ref.1, bf16[1,8]{1,0:T(2,128)(2,1)} %prob_ref.1, s32[1,8]{1,0:T(1,128)} %dest_ref.1, bf16[1,3584,1024]{2,1,0:T(8,128)(2,1)} %wg_hbm.1, bf16[1,3584,1024]{2,1,0:T(8,128)(2,1)} %wu_hbm.1, bf16[1,1024,3584]{2,1,0:T(8,128)(2,1)} %wd_hbm.1), custom_call_target="tpu_custom_call" | custom-call | flops 1174405120 | bytes 22020096 | tf_op jit(solution)/shard_map/pallas_call | solution.py:374
  36.3 1.3 %shard_map.87 = (bf16[1,3584]{1,0:T(2,128)(2,1)}, f32[1,8]{1,0:T(1,128)}) custom-call(f32[2,16,128]{2,1,0:T(8,128)} %shard_map.86.total_ref), custom_call_target="tpu_custom_call" | custom-call | tf_op jit(solution)/shard_map/pallas_call | solution.py:420

commit v4 on v3

--- a/solution.py
+++ b/solution.py
@@ -9,9 +9,10 @@
 
 MESH = pl.DeviceIdType.MESH
 LANES = 128
-TILE = 256
+TILE = 512
+COLUMNS = 256
 HALVES = 2
-PIECES = 2
+PIECES = 4
 
 
 def expert_terms(rows_x, rows_dy, rows_gate, weight_gate, weight_up, weight_down):
@@ -163,15 +164,27 @@
         src, dst = ((wg_hbm, wg), (wu_hbm, wu), (wd_hbm, wd))[which]
         if which == 2:
             step = TILE // PIECES
-            at = (pl.ds(pl.multiple_of(i * TILE + p * step, step), step), slice(None))
+            at = (pl.ds(i * TILE + p * step, step), slice(None))
         else:
             step = width // PIECES
-            at = (pl.ds(p * step, step), pl.ds(pl.multiple_of(i * TILE, TILE), TILE))
+            at = (pl.ds(p * step, step), pl.ds(i * TILE, TILE))
         return pltpu.make_async_copy(src.at[(0, *at)], dst.at[at], w_sem.at[which, i, p])
 
     def await_load(which, i):
         for p in range(PIECES):
             load(which, i, p).wait()
+
+    waiting = [
+        (which, i, p)
+        for group in ((0, 1), (2,))
+        for i in range(units // TILE)
+        for which in group
+        for p in range(PIECES)
+    ]
+
+    def issue(number):
+        for _ in range(min(number, len(waiting))):
+            load(*waiting.pop(0)).start()
 
     barrier = pltpu.get_barrier_semaphore()
     for k in range(1, nodes):
@@ -180,11 +193,7 @@
         )
     for j, side in peers:
         pl.semaphore_signal(barrier, inc=1, device_id=ahead(j, side), device_id_type=MESH)
-    for group in ((0, 1), (2,)):
-        for i in range(units // TILE):
-            for which in group:
-                for p in range(PIECES):
-                    load(which, i, p).start()
+    issue(4)
 
     experts = prob_ref.shape[1]
     for ref, gath in ((tok_ref, gath_x), (dy_ref, gath_dy)):
@@ -232,10 +241,13 @@
             send(gath.at[0, 0, 0], gath.at[0, 0, k], zs.at[at, k], zr.at[at, k], to)
         if at == 0:
             across(0)
+    issue(3)
     for k in range(1, nodes):
         await_recv(gath_x.at[0, 0, k], zs.at[0, 0], zr.at[0, k])
         across(k)
+        issue(1)
     sideways(0)
+    issue(1)
     for k in range(1, nodes):
         await_recv(gath_dy.at[0, 0, k], zs.at[0, 0], zr.at[1, k])
     for j, side in peers:
@@ -246,10 +258,13 @@
             dr.at[j, side],
             ahead(j, side),
         )
+    issue(2)
     for j in range(1, chips):
         for k in range(nodes):
             await_recv(gath_x.at[j, 0, k], cs.at[0, 0], cr.at[j, k])
         sideways(j)
+        issue(1)
+    issue(len(waiting))
     for j in range(chips):
         await_recv(gath_x.at[j, 1], ks.at[0], kr.at[j])
 
@@ -278,23 +293,21 @@
     here = dest == node.astype(f32)
     prob = jnp.where(here, prob, 0.0)
 
-    def forward_tile(i, _):
+    for i in range(units // TILE):
         await_load(0, i)
         await_load(1, i)
-        at = pl.ds(pl.multiple_of(i * TILE, TILE), TILE)
+        at = pl.ds(i * TILE, TILE)
         pre_g[:, at] = jnp.dot(rows_ref[...], wg[:, at], preferred_element_type=f32)
         pre_u[:, at] = jnp.dot(rows_ref[...], wu[:, at], preferred_element_type=f32)
-        return 0
-
-    lax.fori_loop(0, units // TILE, forward_tile, 0)
 
     for j, side in peers:
         await_recv(gath_dy.at[j, side], ds.at[0, 0], dr.at[j, side])
     to_rows(gath_dy)
 
-    def hidden_tile(i, gate_sum):
+    gate_sum = jnp.zeros((count, 1), f32)
+    for i in range(units // TILE):
         await_load(2, i)
-        at = pl.ds(pl.multiple_of(i * TILE, TILE), TILE)
+        at = pl.ds(i * TILE, TILE)
         pre_gate, pre_up = pre_g[:, at], pre_u[:, at]
         back_hidden = dot_nt(rows_ref[...], wd[at, :])
         logistic = jax.nn.sigmoid(pre_gate)
@@ -303,9 +316,6 @@
         scaled = prob * back_hidden
         dg[:, at] = (scaled * pre_up * logistic * (1.0 + pre_gate * (1.0 - logistic))).astype(bf16)
         du[:, at] = (scaled * swished).astype(bf16)
-        return gate_sum
-
-    gate_sum = lax.fori_loop(0, units // TILE, hidden_tile, jnp.zeros((count, 1), f32))
     gate_row = jnp.where(mine & here, gate_sum, 0.0)
     gate_high = gate_row.astype(bf16).astype(f32)
 
@@ -318,16 +328,13 @@
                 value = gate_row - gate_high
             terms[pl.ds(extra, count, stride=padded), :] = value
 
-        def input_tile(i, _):
-            at = pl.ds(pl.multiple_of(h * half + i * TILE, TILE), TILE)
+        for i in range(half // COLUMNS):
+            at = pl.ds(h * half + i * COLUMNS, COLUMNS)
             block = dot_nt(dg[...], wg[at, :]) + dot_nt(du[...], wu[at, :])
-            for c in range(TILE // LANES):
-                terms[pl.ds(i * (TILE // LANES) + c, count, stride=padded), :] = block[
+            for c in range(COLUMNS // LANES):
+                terms[pl.ds(i * (COLUMNS // LANES) + c, count, stride=padded), :] = block[
                     :, c * LANES : (c + 1) * LANES
                 ]
-            return 0
-
-        lax.fori_loop(0, half // TILE, input_tile, 0)
         for j in range(chips):
             for side in range(2):
                 at = (j * 2 + side) * nodes * padded
@@ -450,7 +457,8 @@
         tokens.shape[0] == 1
         and gate_prob.shape[1] == locals_
         and locals_ % 2 == 0
-        and width % (HALVES * TILE) == 0
+        and width % (HALVES * COLUMNS) == 0
+        and width % (16 * PIECES) == 0
         and units % TILE == 0
         and weights + rows < 40 << 20
     )

time: 38 us -> 36.1 us (0.950)
  Pallas kernels: 37 us -> 35.1 us
    pallas_call x1, Pallas kernels: 35.7 us -> 33.8 us  [fused(): pl.pallas_call(functools.partial(fused_kernel, nodes, locals_), out_shape...]
where the time goes in v4:
time: 36.1 us; the launch traced here: 35.8 us
  Pallas kernels  35.1 us (97%)
  between operations  0.64 us (2%)
    pallas_call x1, Pallas kernels, fused(): pl.pallas_call(functools.partial(fused_kernel, nodes, locals_), out_shape...  33.8 us
    pallas_call x1, Pallas kernels, fused(): pl.pallas_call(round_kernel, out_shape=(jax.ShapeDtypeStruct((1, width),...  1.34 us

profile of v4, /device:TPU:0, one launch (start us, length us, event | category | flops | bytes accessed | tf_op | source)
XLA Modules:
  0.0 35.8 jit_solution(186427972954032408)
XLA Ops:
  0.6 33.8 %shard_map.86.total_ref = f32[2,16,128]{2,1,0:T(8,128)} custom-call(bf16[1,3584]{1,0:T(2,128)(2,1)} %tok_ref.1, bf16[1,3584]{1,0:T(2,128)(2,1)} %dy_ref.1, bf16[1,8]{1,0:T(2,128)(2,1)} %prob_ref.1, s32[1,8]{1,0:T(1,128)} %dest_ref.1, bf16[1,3584,1024]{2,1,0:T(8,128)(2,1)} %wg_hbm.1, bf16[1,3584,1024]{2,1,0:T(8,128)(2,1)} %wu_hbm.1, bf16[1,1024,3584]{2,1,0:T(8,128)(2,1)} %wd_hbm.1), custom_call_target="tpu_custom_call" | custom-call | flops 1174405120 | bytes 22020096 | tf_op jit(solution)/shard_map/pallas_call | solution.py:381
  34.4 1.3 %shard_map.87 = (bf16[1,3584]{1,0:T(2,128)(2,1)}, f32[1,8]{1,0:T(1,128)}) custom-call(f32[2,16,128]{2,1,0:T(8,128)} %shard_map.86.total_ref), custom_call_target="tpu_custom_call" | custom-call | tf_op jit(solution)/shard_map/pallas_call | solution.py:427

commit v5 on v4

--- a/solution.py
+++ b/solution.py
@@ -174,17 +174,13 @@
         for p in range(PIECES):
             load(which, i, p).wait()
 
-    waiting = [
+    pieces = [
         (which, i, p)
         for group in ((0, 1), (2,))
         for i in range(units // TILE)
         for which in group
         for p in range(PIECES)
     ]
-
-    def issue(number):
-        for _ in range(min(number, len(waiting))):
-            load(*waiting.pop(0)).start()
 
     barrier = pltpu.get_barrier_semaphore()
     for k in range(1, nodes):
@@ -193,7 +189,8 @@
         )
     for j, side in peers:
         pl.semaphore_signal(barrier, inc=1, device_id=ahead(j, side), device_id_type=MESH)
-    issue(4)
+    for piece in pieces:
+        load(*piece).start()
 
     experts = prob_ref.shape[1]
     for ref, gath in ((tok_ref, gath_x), (dy_ref, gath_dy)):
@@ -241,13 +238,10 @@
             send(gath.at[0, 0, 0], gath.at[0, 0, k], zs.at[at, k], zr.at[at, k], to)
         if at == 0:
             across(0)
-    issue(3)
     for k in range(1, nodes):
         await_recv(gath_x.at[0, 0, k], zs.at[0, 0], zr.at[0, k])
         across(k)
-        issue(1)
     sideways(0)
-    issue(1)
     for k in range(1, nodes):
         await_recv(gath_dy.at[0, 0, k], zs.at[0, 0], zr.at[1, k])
     for j, side in peers:
@@ -258,13 +252,10 @@
             dr.at[j, side],
             ahead(j, side),
         )
-    issue(2)
     for j in range(1, chips):
         for k in range(nodes):
             await_recv(gath_x.at[j, 0, k], cs.at[0, 0], cr.at[j, k])
         sideways(j)
-        issue(1)
-    issue(len(waiting))
     for j in range(chips):
         await_recv(gath_x.at[j, 1], ks.at[0], kr.at[j])
 
@@ -348,6 +339,11 @@
                         back(j, side),
                     )
 
+    def drain():
+        while sent:
+            sent.pop(0).wait_send()
+
+    drain()
     for h in range(HALVES):
         total = send1[h, 0, 0].astype(f32)
         for j, side in peers:
@@ -364,8 +360,7 @@
             await_recv(recv2.at[h, k], bs.at[h, 0], br.at[h, k])
             total = total + recv2[h, k]
         out_ref[h] = total
-    for copy in sent:
-        copy.wait_send()
+    drain()
 
 
 def fused(nodes, locals_, tokens, out_grad, gate_prob, dest_node, w_gate, w_up, w_down):

time: 36.1 us -> 36 us (level)
  no operation moved by 1% of the time
where the time goes in v5:
time: 36 us; the launch traced here: 35.7 us
  Pallas kernels  35 us (97%)
  between operations  0.64 us (2%)
    pallas_call x1, Pallas kernels, fused(): pl.pallas_call(functools.partial(fused_kernel, nodes, locals_), out_shape...  33.7 us
    pallas_call x1, Pallas kernels, fused(): pl.pallas_call(round_kernel, out_shape=(jax.ShapeDtypeStruct((1, width),...  1.34 us

profile of v5, /device:TPU:0, one launch (start us, length us, event | category | flops | bytes accessed | tf_op | source)
XLA Modules:
  0.0 35.7 jit_solution(12098778138501171455)
XLA Ops:
  0.6 33.7 %shard_map.86.total_ref = f32[2,16,128]{2,1,0:T(8,128)} custom-call(bf16[1,3584]{1,0:T(2,128)(2,1)} %tok_ref.1, bf16[1,3584]{1,0:T(2,128)(2,1)} %dy_ref.1, bf16[1,8]{1,0:T(2,128)(2,1)} %prob_ref.1, s32[1,8]{1,0:T(1,128)} %dest_ref.1, bf16[1,3584,1024]{2,1,0:T(8,128)(2,1)} %wg_hbm.1, bf16[1,3584,1024]{2,1,0:T(8,128)(2,1)} %wu_hbm.1, bf16[1,1024,3584]{2,1,0:T(8,128)(2,1)} %wd_hbm.1), custom_call_target="tpu_custom_call" | custom-call | flops 1174405120 | bytes 22020096 | tf_op jit(solution)/shard_map/pallas_call | solution.py:376
  34.3 1.3 %shard_map.87 = (bf16[1,3584]{1,0:T(2,128)(2,1)}, f32[1,8]{1,0:T(1,128)}) custom-call(f32[2,16,128]{2,1,0:T(8,128)} %shard_map.86.total_ref), custom_call_target="tpu_custom_call" | custom-call | tf_op jit(solution)/shard_map/pallas_call | solution.py:422
